TPU v7x, 32 devices: a whole 2x2x4 slice. The times are simulated.
32 devices in a mesh: grp: 2 (over x), leaf: 8 (over z, y), sub: 2 (over core).
Axes of the slice: x: 2, y: 2, z: 4, core: 2. Of those that a mesh axis runs over, the one named last changes fastest.
Arguments:
- right_side: float32 [512, 2048], P(('grp', 'leaf', 'sub')), parts along dimension 0, may hold values from -24 to 24, as said below
- first_guess: float32 [512, 2048], P(('grp', 'leaf', 'sub')), parts along dimension 0, may hold values from -3 to 3
- couple: bfloat16 [512, 64, 384], P(('grp', 'leaf', 'sub')), parts along dimension 0, may hold values from -0.75 to 0.75
- send_lists: int32 [32, 2, 4], P(('grp', 'leaf', 'sub')), parts along dimension 0, may hold values from -1 to 15, as said below
- neighbours: int32 [512, 6], P(('grp', 'leaf', 'sub')), parts along dimension 0, may hold values from -1 to 23, as said below
Outputs:
- solution: float32 [512, 2048], P(('grp', 'leaf', 'sub')), parts along dimension 0
- residual: float32 [512, 2048], P(('grp', 'leaf', 'sub')), parts along dimension 0
There are 2 independent parts, one for each index of `grp`. A program takes and returns all parts, laid end to end along the dimension named above; each array names one. Nothing has to cross between parts.
Inputs may be any that keep to these rules, and one draw needn't show every extreme that they name: `right_side`: rows rise in scale along the element order. `send_lists`: for device d of a part and direction 0 (toward device d + 1) or 1 (toward device d - 1): distinct local element indices in the live slots, which come first, and -1 after them. The first device sends nothing in direction 1, the last nothing in direction 0; some device fills all 4 slots in direction 0 and the device after it all 4 in direction 1. `neighbours`: positions below 16 are the device's own elements, 16 + s the live slot s received from the previous device, 20 + s the live slot s received from the next device; -1 marks a face on the band's boundary.
All inputs are finite; a program needn't handle non-finite values.
Results may differ from a plain program's by a relative error of at most 0.034.
Values may be sent and summed in bfloat16 or wider, within the bound.
A program may use at most 64 MiB of HBM per device.

v0:
```python
import jax
import jax.numpy as jnp
from jax import lax
from jax.sharding import PartitionSpec as P

DOF = 64
FACES = 6
RHS = 32
SSTEP = 3
CYCLES = 4


def from_behind(value, axis, steps):
    count = lax.axis_size(axis)
    first, last = (max(0, -steps), min(count, count - steps))
    return lax.ppermute(value, axis, [(source, source + steps) for source in range(first, last)])


def couple_apply(vector_field, couple, send_lists, neighbours):
    local_count = vector_field.shape[0]
    slot_count = send_lists.shape[2]
    row_width = vector_field.shape[1]
    halves = vector_field.astype(jnp.bfloat16)
    own_lists = send_lists[0]
    chosen = jnp.take(halves, jnp.maximum(own_lists, 0).reshape(-1), axis=0).reshape(
        2, slot_count, row_width
    )
    chosen = jnp.where(own_lists[:, :, None] >= 0, chosen, jnp.zeros_like(chosen))
    forward = chosen[0]
    backward = chosen[1]
    before_blocks = from_behind(forward, ("leaf", "sub"), 1)
    after_blocks = from_behind(backward, ("leaf", "sub"), -1)
    zero_block = jnp.zeros((1, row_width), jnp.bfloat16)
    extended = jnp.concatenate([halves, before_blocks, after_blocks, zero_block], axis=0)
    positions = jnp.where(neighbours < 0, local_count + 2 * slot_count, neighbours).reshape(-1)
    gathered = jnp.take(extended, positions, axis=0).reshape(local_count, FACES * DOF, RHS)
    product = jnp.einsum("eik,ekr->eir", couple, gathered, preferred_element_type=jnp.float32)
    return product.reshape(local_count, DOF * RHS)


def to_columns(vector_field):
    return vector_field.reshape(-1, RHS)


def basis_sums(stacked):
    partial_sum = jnp.dot(
        stacked.T, stacked, precision=lax.Precision.HIGHEST, preferred_element_type=jnp.float32
    )
    total_sum = lax.psum(partial_sum, ("leaf", "sub"))
    return (total_sum[: SSTEP * RHS, : SSTEP * RHS], total_sum[: SSTEP * RHS, SSTEP * RHS :])


def shards(right_side, first_guess, couple, send_lists, neighbours):
    solution = first_guess
    residual = right_side - first_guess + couple_apply(first_guess, couple, send_lists, neighbours)
    for repeat in range(CYCLES):
        krylov_blocks = [residual]
        for degree in range(SSTEP):
            krylov_blocks.append(couple_apply(krylov_blocks[-1], couple, send_lists, neighbours))
        images = [
            krylov_blocks[order_index] - krylov_blocks[order_index + 1]
            for order_index in range(SSTEP)
        ]
        stacked = jnp.concatenate(
            [to_columns(image_block) for image_block in images] + [to_columns(residual)], axis=1
        )
        square_block, right_block = basis_sums(stacked)
        factor = jnp.linalg.cholesky(square_block)
        coeffs = jax.scipy.linalg.cho_solve((factor, True), right_block)
        krylov = jnp.concatenate(
            [to_columns(basis_block) for basis_block in krylov_blocks[:SSTEP]], axis=1
        )
        solution = solution + jnp.dot(
            krylov, coeffs, precision=lax.Precision.HIGHEST, preferred_element_type=jnp.float32
        ).reshape(solution.shape)
        residual = residual - jnp.dot(
            stacked[:, : SSTEP * RHS],
            coeffs,
            precision=lax.Precision.HIGHEST,
            preferred_element_type=jnp.float32,
        ).reshape(residual.shape)
    return (solution, residual)


def solution(mesh):
    placed = (
        P(("grp", "leaf", "sub"), None),
        P(("grp", "leaf", "sub"), None),
        P(("grp", "leaf", "sub"), None, None),
        P(("grp", "leaf", "sub"), None, None),
        P(("grp", "leaf", "sub"), None),
    )
    return jax.shard_map(
        shards,
        mesh=mesh,
        in_specs=placed,
        out_specs=(P(("grp", "leaf", "sub"), None), P(("grp", "leaf", "sub"), None)),
        check_vma=False,
    )
```

profile of v0, /device:TPU:8, one launch (start us, length us, event | category | flops | bytes accessed | tf_op | source)
XLA Modules:
  0.0 679.5 jit_solution(5330621828256337347)
XLA Ops:
  10.5 1.9 collective-permute-start
  12.4 4.5 collective-permute-start.1
  22.6 2.6 collective-permute-start.2
  25.2 3.8 collective-permute-start.3
  32.3 2.2 reshape.259
  37.1 2.5 collective-permute-start.4
  39.6 4.0 collective-permute-start.5
  46.7 2.2 reshape.262
  51.0 2.5 collective-permute-start.6
  53.5 4.2 collective-permute-start.7
  62.2 2.2 reshape.265
  66.7 87.3 %all-reduce.5.cloned.1.call-done = f32[128,128]{0,1:T(8,128)} async-done(((f32[128,128]{0,1:T(8,128)}), f32[128,128]{0,1:T(8,128)}) %all-reduce.5.cloned.1.call-update) | async-done | bytes 65552 | tf_op jit(solution)/shard_map/psum | solution.py:49
  155.8 8.8 %cholesky.74 = f32[96,96]{1,0:T(8,128)S(1)} custom-call(f32[96,96]{1,0:T(8,128)S(1)} %fusion.103), custom_call_target="Cholesky" | custom-call | tf_op jit(solution)/shard_map/jit(cholesky)/cholesky | solution.py:68
  165.9 7.4 %custom-call.10 = f32[1,96,96]{1,2,0:T(8,128)S(1)} custom-call(f32[1,96,96]{2,1,0:T(8,128)S(1)} %fusion.80), custom_call_target="InvertDiagBlocksLowerTriangular" | custom-call | tf_op jit(solution)/shard_map/jit(_cho_solve)/triangular_solve | solution.py:69
  176.5 1.9 collective-permute-start.8
  178.5 4.5 collective-permute-start.9
  189.5 1.9 collective-permute-start.10
  191.5 4.9 collective-permute-start.11
  199.4 2.2 reshape.274
  209.0 4.5 collective-permute-start.13
  219.4 2.2 reshape.277
  224.8 86.2 %all-reduce.7.cloned.1.call-done = f32[128,128]{0,1:T(8,128)} async-done(((f32[128,128]{0,1:T(8,128)}), f32[128,128]{0,1:T(8,128)}) %all-reduce.7.cloned.1.call-update) | async-done | bytes 65552 | tf_op jit(solution)/shard_map/psum | solution.py:49
  312.7 8.8 %cholesky.85 = f32[96,96]{1,0:T(8,128)S(1)} custom-call(f32[96,96]{1,0:T(8,128)S(1)} %fusion.98), custom_call_target="Cholesky" | custom-call | tf_op jit(solution)/shard_map/jit(cholesky)/cholesky | solution.py:68
  322.8 7.4 %custom-call.11 = f32[1,96,96]{1,2,0:T(8,128)S(1)} custom-call(f32[1,96,96]{2,1,0:T(8,128)S(1)} %fusion.81), custom_call_target="InvertDiagBlocksLowerTriangular" | custom-call | tf_op jit(solution)/shard_map/jit(_cho_solve)/triangular_solve | solution.py:69
  334.1 2.1 collective-permute-start.14
  336.2 4.5 collective-permute-start.15
  344.1 2.2 reshape.283
  350.7 1.9 collective-permute-start.16
  352.6 4.5 collective-permute-start.17
  360.5 2.2 reshape.286
  370.2 4.5 collective-permute-start.19
  380.9 2.2 reshape.289
  386.5 85.9 %all-reduce.9.cloned.1.call-done = f32[128,128]{0,1:T(8,128)} async-done(((f32[128,128]{0,1:T(8,128)}), f32[128,128]{0,1:T(8,128)}) %all-reduce.9.cloned.1.call-update) | async-done | bytes 65552 | tf_op jit(solution)/shard_map/psum | solution.py:49
  474.1 8.8 %cholesky.96 = f32[96,96]{1,0:T(8,128)S(1)} custom-call(f32[96,96]{1,0:T(8,128)S(1)} %fusion.93), custom_call_target="Cholesky" | custom-call | tf_op jit(solution)/shard_map/jit(cholesky)/cholesky | solution.py:68
  484.3 7.4 %custom-call.12 = f32[1,96,96]{1,2,0:T(8,128)S(1)} custom-call(f32[1,96,96]{2,1,0:T(8,128)S(1)} %fusion.82), custom_call_target="InvertDiagBlocksLowerTriangular" | custom-call | tf_op jit(solution)/shard_map/jit(_cho_solve)/triangular_solve | solution.py:69
  495.0 1.9 collective-permute-start.20
  496.9 4.5 collective-permute-start.21
  505.4 2.2 reshape.295
  515.0 1.9 collective-permute-start.22
  517.0 4.9 collective-permute-start.23
  529.3 2.2 reshape.298
  539.1 4.5 collective-permute-start.25
  546.4 2.0 copy.147
  554.9 2.5 reshape.301
  560.1 2.2 fusion.48
  566.2 82.3 %all-reduce.11.cloned.1.call-done = f32[128,128]{0,1:T(8,128)} async-done(((f32[128,128]{0,1:T(8,128)}), f32[128,128]{0,1:T(8,128)}) %all-reduce.11.cloned.1.call-update) | async-done | bytes 65552 | tf_op jit(solution)/shard_map/psum | solution.py:49
  650.3 8.8 %cholesky.107 = f32[96,96]{1,0:T(8,128)S(1)} custom-call(f32[96,96]{1,0:T(8,128)S(1)} %fusion.88), custom_call_target="Cholesky" | custom-call | tf_op jit(solution)/shard_map/jit(cholesky)/cholesky | solution.py:68
  660.4 7.4 %custom-call.13 = f32[1,96,96]{1,2,0:T(8,128)S(1)} custom-call(f32[1,96,96]{2,1,0:T(8,128)S(1)} %fusion.83), custom_call_target="InvertDiagBlocksLowerTriangular" | custom-call | tf_op jit(solution)/shard_map/jit(_cho_solve)/triangular_solve | solution.py:69
  (460 shorter events, 148.3 us)
Async XLA Ops:
  7.2 146.9 %all-reduce.5.cloned.1.call-start = ((), (), s32[]{:S(2)}) async-start(), calls=%async_computation | async-start | bytes 131072 | tf_op jit(solution)/shard_map/psum | solution.py:49
  8.0 42.9 %copy-start.57 = (pred[2,4]{1,0:T(4,128)(4,1)}, pred[2,4]{1,0:T(4,128)(4,1)S(1)}, u32[]{:S(2)}) copy-start(pred[2,4]{1,0:T(4,128)(4,1)S(1)} %compare_bitcast_fusion) | copy-start | bytes 28
  8.8 42.0 %copy-start.63 = (pred[8]{0:T(512)(128)(4,1)}, pred[8]{0:T(512)(128)(4,1)S(1)}, u32[]{:S(2)}) copy-start(pred[8]{0:T(512)(128)(4,1)S(1)} %compare_and_fusion.1) | copy-start | bytes 28
  8.8 27.5 %copy-start.78 = (s32[1024]{0:T(1024)}, s32[1024]{0:T(1024)S(1)}, u32[]{:S(2)}) copy-start(s32[1024]{0:T(1024)S(1)} %pad_clamp_fusion.1) | copy-start | bytes 12292
  10.5 7.5 %collective-permute-start = (bf16[4,2048]{1,0:T(4,128)(2,1)S(1)}, bf16[4,2048]{1,0:T(4,128)(2,1)S(1)}, u32[]{:S(2)}, u32[]{:S(2)}) collective-permute-start(bf16[4,2048]{1,0:T(4,128)(2,1)S(1)} %get-tuple-element.54), channel_id=1, source_target_pairs={{0,1},{1,2},{2,3},{3,4},{4,5},{5,6},{6,7},{7,8},{8,9},{9,10},{10,1... | collective-permute-start | bytes 49160 | tf_op jit(solution)/shard_map/ppermute | solution.py:16
  12.4 6.0 collective-permute-start.1
  17.9 43.5 %copy-start.69 = (pred[96]{0:T(512)(128)(4,1)}, pred[96]{0:T(512)(128)(4,1)S(1)}, u32[]{:S(2)}) copy-start(pred[96]{0:T(512)(128)(4,1)S(1)} %compare_and_fusion) | copy-start | bytes 292
  18.0 42.3 %copy-start.47 = (bf16[25]{0:T(256)(128)(2,1)}, bf16[25]{0:T(256)(128)(2,1)S(1)}, u32[]{:S(2)}) copy-start(bf16[25]{0:T(256)(128)(2,1)S(1)} %pad.91.clone) | copy-start | bytes 154
  22.6 6.5 collective-permute-start.2
  25.2 5.3 collective-permute-start.3
  37.1 6.5 collective-permute-start.4
  39.6 5.4 collective-permute-start.5
  51.0 9.3 %collective-permute-start.6 = (bf16[4,2048]{1,0:T(4,128)(2,1)S(1)}, bf16[4,2048]{1,0:T(4,128)(2,1)S(1)}, u32[]{:S(2)}, u32[]{:S(2)}) collective-permute-start(bf16[4,2048]{1,0:T(4,128)(2,1)S(1)} %get-tuple-element.48), channel_id=1, source_target_pairs={{0,1},{1,2},{2,3},{3,4},{4,5},{5,6},{6,7},{7,8},{8,9},{9,10},{10,1... | collective-permute-start | bytes 49160 | tf_op jit(solution)/shard_map/ppermute | solution.py:16
  53.5 6.8 %collective-permute-start.7 = (bf16[4,2048]{1,0:T(4,128)(2,1)S(1)}, bf16[4,2048]{1,0:T(4,128)(2,1)S(1)}, u32[]{:S(2)}, u32[]{:S(2)}) collective-permute-start(bf16[4,2048]{1,0:T(4,128)(2,1)S(1)} %get-tuple-element.49), channel_id=1, source_target_pairs={{1,0},{2,1},{3,2},{4,3},{5,4},{6,5},{7,6},{8,7},{9,8},{10,9},{11,1... | collective-permute-start | bytes 49160 | tf_op jit(solution)/shard_map/ppermute | solution.py:16
  66.7 109.6 %copy-start.64 = (pred[8]{0:T(512)(128)(4,1)S(1)}, pred[8]{0:T(512)(128)(4,1)}, u32[]{:S(2)}) copy-start(pred[8]{0:T(512)(128)(4,1)} %copy-done.63) | copy-start | bytes 28
  66.7 109.7 %copy-start.58 = (pred[2,4]{1,0:T(4,128)(4,1)S(1)}, pred[2,4]{1,0:T(4,128)(4,1)}, u32[]{:S(2)}) copy-start(pred[2,4]{1,0:T(4,128)(4,1)} %copy-done.57) | copy-start | bytes 28
  66.7 244.3 %all-reduce.7.cloned.1.call-start = ((), (), s32[]{:S(2)}) async-start(), calls=%async_computation.1 | async-start | bytes 131072 | tf_op jit(solution)/shard_map/psum | solution.py:49
  154.9 29.6 %copy-start.48 = (bf16[25]{0:T(256)(128)(2,1)S(1)}, bf16[25]{0:T(256)(128)(2,1)}, u32[]{:S(2)}) copy-start(bf16[25]{0:T(256)(128)(2,1)} %copy-done.47) | copy-start | bytes 154
  176.5 6.5 collective-permute-start.8
  178.5 6.0 collective-permute-start.9
  189.5 6.9 %collective-permute-start.10 = (bf16[4,2048]{1,0:T(4,128)(2,1)S(1)}, bf16[4,2048]{1,0:T(4,128)(2,1)S(1)}, u32[]{:S(2)}, u32[]{:S(2)}) collective-permute-start(bf16[4,2048]{1,0:T(4,128)(2,1)S(1)} %get-tuple-element.44), channel_id=1, source_target_pairs={{0,1},{1,2},{2,3},{3,4},{4,5},{5,6},{6,7},{7,8},{8,9},{9,10},{10,1... | collective-permute-start | bytes 49160 | tf_op jit(solution)/shard_map/ppermute | solution.py:16
  191.5 6.0 collective-permute-start.11
  207.1 10.4 %collective-permute-start.12 = (bf16[4,2048]{1,0:T(4,128)(2,1)}, bf16[4,2048]{1,0:T(4,128)(2,1)S(1)}, u32[]{:S(2)}, u32[]{:S(2)}) collective-permute-start(bf16[4,2048]{1,0:T(4,128)(2,1)} %get-tuple-element.42), channel_id=1, source_target_pairs={{0,1},{1,2},{2,3},{3,4},{4,5},{5,6},{6,7},{7,8},{8,9},{9,10},{10,1... | collective-permute-start | bytes 49160 | tf_op jit(solution)/shard_map/ppermute | solution.py:16
  209.0 8.4 %collective-permute-start.13 = (bf16[4,2048]{1,0:T(4,128)(2,1)S(1)}, bf16[4,2048]{1,0:T(4,128)(2,1)S(1)}, u32[]{:S(2)}, u32[]{:S(2)}) collective-permute-start(bf16[4,2048]{1,0:T(4,128)(2,1)S(1)} %get-tuple-element.43), channel_id=1, source_target_pairs={{1,0},{2,1},{3,2},{4,3},{5,4},{6,5},{7,6},{8,7},{9,8},{10,9},{11,1... | collective-permute-start | bytes 49160 | tf_op jit(solution)/shard_map/ppermute | solution.py:16
  224.7 109.1 %copy-start.66 = (pred[8]{0:T(512)(128)(4,1)S(1)}, pred[8]{0:T(512)(128)(4,1)}, u32[]{:S(2)}) copy-start(pred[8]{0:T(512)(128)(4,1)} %copy-done.63) | copy-start | bytes 28
  224.8 109.2 %copy-start.60 = (pred[2,4]{1,0:T(4,128)(4,1)S(1)}, pred[2,4]{1,0:T(4,128)(4,1)}, u32[]{:S(2)}) copy-start(pred[2,4]{1,0:T(4,128)(4,1)} %copy-done.57) | copy-start | bytes 28
  224.8 247.6 %all-reduce.9.cloned.1.call-start = ((), (), s32[]{:S(2)}) async-start(), calls=%async_computation.2 | async-start | bytes 131072 | tf_op jit(solution)/shard_map/psum | solution.py:49
  311.8 30.4 %copy-start.51 = (bf16[25]{0:T(256)(128)(2,1)S(1)}, bf16[25]{0:T(256)(128)(2,1)}, u32[]{:S(2)}) copy-start(bf16[25]{0:T(256)(128)(2,1)} %copy-done.47) | copy-start | bytes 154
  334.1 6.6 collective-permute-start.14
  336.2 6.0 collective-permute-start.15
  350.7 6.5 collective-permute-start.16
  352.6 6.0 collective-permute-start.17
  368.2 10.7 %collective-permute-start.18 = (bf16[4,2048]{1,0:T(4,128)(2,1)}, bf16[4,2048]{1,0:T(4,128)(2,1)S(1)}, u32[]{:S(2)}, u32[]{:S(2)}) collective-permute-start(bf16[4,2048]{1,0:T(4,128)(2,1)} %get-tuple-element.36), channel_id=1, source_target_pairs={{0,1},{1,2},{2,3},{3,4},{4,5},{5,6},{6,7},{7,8},{8,9},{9,10},{10,1... | collective-permute-start | bytes 49160 | tf_op jit(solution)/shard_map/ppermute | solution.py:16
  370.2 8.8 %collective-permute-start.19 = (bf16[4,2048]{1,0:T(4,128)(2,1)S(1)}, bf16[4,2048]{1,0:T(4,128)(2,1)S(1)}, u32[]{:S(2)}, u32[]{:S(2)}) collective-permute-start(bf16[4,2048]{1,0:T(4,128)(2,1)S(1)} %get-tuple-element.37), channel_id=1, source_target_pairs={{1,0},{2,1},{3,2},{4,3},{5,4},{6,5},{7,6},{8,7},{9,8},{10,9},{11,1... | collective-permute-start | bytes 49160 | tf_op jit(solution)/shard_map/ppermute | solution.py:16
  385.0 109.0 %copy-start.6 = (f32[16,2048]{1,0:T(8,128)S(1)}, f32[16,2048]{1,0:T(8,128)}, u32[]{:S(2)}) copy-start(f32[16,2048]{1,0:T(8,128)} %get-tuple-element.9) | copy-start | bytes 393220
  386.2 108.6 %copy-start.68 = (pred[8]{0:T(512)(128)(4,1)S(1)}, pred[8]{0:T(512)(128)(4,1)}, u32[]{:S(2)}) copy-start(pred[8]{0:T(512)(128)(4,1)} %copy-done.63) | copy-start | bytes 28
  386.2 108.7 %copy-start.62 = (pred[2,4]{1,0:T(4,128)(4,1)S(1)}, pred[2,4]{1,0:T(4,128)(4,1)}, u32[]{:S(2)}) copy-start(pred[2,4]{1,0:T(4,128)(4,1)} %copy-done.57) | copy-start | bytes 28
  386.2 262.4 %all-reduce.11.cloned.1.call-start = ((), (), s32[]{:S(2)}) async-start(), calls=%async_computation.3 | async-start | bytes 131072 | tf_op jit(solution)/shard_map/psum | solution.py:49
  473.2 28.2 %copy-start.13 = (f32[1024,32]{0,1:T(8,128)S(1)}, f32[1024,32]{0,1:T(8,128)}, u32[]{:S(2)}) copy-start(f32[1024,32]{0,1:T(8,128)} %copy-done.12) | copy-start | bytes 393220
  495.0 8.5 %collective-permute-start.20 = (bf16[4,2048]{1,0:T(4,128)(2,1)S(1)}, bf16[4,2048]{1,0:T(4,128)(2,1)S(1)}, u32[]{:S(2)}, u32[]{:S(2)}) collective-permute-start(bf16[4,2048]{1,0:T(4,128)(2,1)S(1)} %get-tuple-element.34), channel_id=1, source_target_pairs={{0,1},{1,2},{2,3},{3,4},{4,5},{5,6},{6,7},{7,8},{8,9},{9,10},{10,1... | collective-permute-start | bytes 49160 | tf_op jit(solution)/shard_map/ppermute | solution.py:16
  496.9 6.6 collective-permute-start.21
  515.0 12.4 %collective-permute-start.22 = (bf16[4,2048]{1,0:T(4,128)(2,1)S(1)}, bf16[4,2048]{1,0:T(4,128)(2,1)S(1)}, u32[]{:S(2)}, u32[]{:S(2)}) collective-permute-start(bf16[4,2048]{1,0:T(4,128)(2,1)S(1)} %get-tuple-element.32), channel_id=1, source_target_pairs={{0,1},{1,2},{2,3},{3,4},{4,5},{5,6},{6,7},{7,8},{8,9},{9,10},{10,1... | collective-permute-start | bytes 49160 | tf_op jit(solution)/shard_map/ppermute | solution.py:16
  517.0 10.5 %collective-permute-start.23 = (bf16[4,2048]{1,0:T(4,128)(2,1)S(1)}, bf16[4,2048]{1,0:T(4,128)(2,1)S(1)}, u32[]{:S(2)}, u32[]{:S(2)}) collective-permute-start(bf16[4,2048]{1,0:T(4,128)(2,1)S(1)} %get-tuple-element.33), channel_id=1, source_target_pairs={{1,0},{2,1},{3,2},{4,3},{5,4},{6,5},{7,6},{8,7},{9,8},{10,9},{11,1... | collective-permute-start | bytes 49160 | tf_op jit(solution)/shard_map/ppermute | solution.py:16
  537.1 15.1 %collective-permute-start.24 = (bf16[4,2048]{1,0:T(4,128)(2,1)}, bf16[4,2048]{1,0:T(4,128)(2,1)}, u32[]{:S(2)}, u32[]{:S(2)}) collective-permute-start(bf16[4,2048]{1,0:T(4,128)(2,1)} %get-tuple-element.30), channel_id=1, source_target_pairs={{0,1},{1,2},{2,3},{3,4},{4,5},{5,6},{6,7},{7,8},{8,9},{9,10},{10,1... | collective-permute-start | bytes 49160 | tf_op jit(solution)/shard_map/ppermute | solution.py:16
  539.1 13.2 %collective-permute-start.25 = (bf16[4,2048]{1,0:T(4,128)(2,1)}, bf16[4,2048]{1,0:T(4,128)(2,1)}, u32[]{:S(2)}, u32[]{:S(2)}) collective-permute-start(bf16[4,2048]{1,0:T(4,128)(2,1)} %get-tuple-element.31), channel_id=1, source_target_pairs={{1,0},{2,1},{3,2},{4,3},{5,4},{6,5},{7,6},{8,7},{9,8},{10,9},{11,1... | collective-permute-start | bytes 49160 | tf_op jit(solution)/shard_map/ppermute | solution.py:16
  563.1 105.7 %copy-start.25 = (f32[1024,32]{0,1:T(8,128)S(1)}, f32[1024,32]{0,1:T(8,128)}, u32[]{:S(2)}) copy-start(f32[1024,32]{0,1:T(8,128)} %copy.168) | copy-start | bytes 393220
  563.1 105.7 %copy-start.33 = (f32[1024,32]{0,1:T(8,128)S(1)}, f32[1024,32]{0,1:T(8,128)}, u32[]{:S(2)}) copy-start(f32[1024,32]{0,1:T(8,128)} %copy-done.32) | copy-start | bytes 393220
  563.1 105.7 %copy-start.35 = (f32[1024,32]{0,1:T(8,128)S(1)}, f32[1024,32]{0,1:T(8,128)}, u32[]{:S(2)}) copy-start(f32[1024,32]{0,1:T(8,128)} %copy-done.34) | copy-start | bytes 393220
  (62 other events, 338.3 us)
Sparse Core Ops, SparseCore 0:
  66.8 87.2 all-reduce.4
  224.9 86.0 all-reduce.6
  386.3 86.0 all-reduce.8
  562.5 86.0 all-reduce.10
where the time goes:
time: 688 us; the launch traced here: 680 us
  waiting for transfers between devices  350 us (51%)
  other arithmetic  104 us (15%)
  local copies, waits for them, and re-layouts  94.6 us (14%)
  starting transfers between devices  85.5 us (12%)
  matrix products  28.9 us (4%)
  between operations  16.5 us (2%)
    psum x4, waiting for transfers between devices, basis_sums(): total_sum = lax.psum(partial_sum, ('leaf', 'sub'))  342 us
    ppermute x26, starting transfers between devices, from_behind(): lax.ppermute(value, axis, [(source, source + steps) for source in range(f...  85.1 us
    another operation x12, other arithmetic, shards(): factor = jnp.linalg.cholesky(square_block)  37.9 us
    another operation x8, other arithmetic, shards(): coeffs = jax.scipy.linalg.cho_solve((factor, True), right_block)  32 us
    reshape x13, local copies, waits for them, and re-layouts, couple_apply(): jnp.take(extended, positions, axis=0).reshape(local_count, FACES * DOF, RHS)  27.4 us
  transfers between devices with their start and end apart: 30, of which 11 were waited for; matrix products, arithmetic and copies ran while one was open for 5% of the time, Pallas kernels for 0%

commit v1 on v0

--- a/solution.py
+++ b/solution.py
@@ -46,7 +46,7 @@
     partial_sum = jnp.dot(
         stacked.T, stacked, precision=lax.Precision.HIGHEST, preferred_element_type=jnp.float32
     )
-    total_sum = lax.psum(partial_sum, ("leaf", "sub"))
+    total_sum = jnp.sum(lax.all_gather(partial_sum, ("leaf", "sub")), axis=0)
     return (total_sum[: SSTEP * RHS, : SSTEP * RHS], total_sum[: SSTEP * RHS, SSTEP * RHS :])
 
 

time: 688 us -> 476 us (0.69)
  the two profiles are of different devices: /device:TPU:8 before, /device:TPU:0 now
where the time goes in v1:
time: 476 us; the launch traced here: 467 us
  waiting for transfers between devices  169 us (36%)
  other arithmetic  101 us (21%)
  local copies, waits for them, and re-layouts  86.8 us (18%)
  starting transfers between devices  67.8 us (14%)
  matrix products  26.2 us (6%)
  between operations  16.4 us (3%)
    all_gather x4, waiting for transfers between devices, basis_sums(): total_sum = jnp.sum(lax.all_gather(partial_sum, ('leaf', 'sub')), axis=0)  153 us
    ppermute x26, starting transfers between devices, from_behind(): lax.ppermute(value, axis, [(source, source + steps) for source in range(f...  67.4 us
    another operation x12, other arithmetic, shards(): factor = jnp.linalg.cholesky(square_block)  37.9 us
    another operation x8, other arithmetic, shards(): coeffs = jax.scipy.linalg.cho_solve((factor, True), right_block)  32.1 us
    reshape x13, local copies, waits for them, and re-layouts, couple_apply(): jnp.take(extended, positions, axis=0).reshape(local_count, FACES * DOF, RHS)  26.4 us
    ppermute x26, waiting for transfers between devices, from_behind(): lax.ppermute(value, axis, [(source, source + steps) for source in range(f...  16.7 us
    dot_general x13, matrix products, couple_apply(): jnp.einsum('eik,ekr->eir', couple, gathered, preferred_element_type=jnp.f...  12.5 us
    gather x13, local copies, waits for them, and re-layouts, couple_apply(): jnp.take(extended, positions, axis=0).reshape(local_count, FACES * DOF, RHS)  12.3 us
  transfers between devices with their start and end apart: 30, of which 13 were waited for; matrix products, arithmetic and copies ran while one was open for 6% of the time, Pallas kernels for 0%

profile of v1, /device:TPU:0, one launch (start us, length us, event | category | flops | bytes accessed | tf_op | source)
XLA Modules:
  0.0 467.4 jit_solution(17120015142865215574)
XLA Ops:
  10.5 2.4 collective-permute-start
  15.2 2.9 collective-permute-done.1
  24.0 4.4 collective-permute-start.2
  29.7 1.8 collective-permute-done.3
  36.5 4.7 %collective-permute-start.4 = (bf16[4,2048]{1,0:T(4,128)(2,1)S(1)}, bf16[4,2048]{1,0:T(4,128)(2,1)S(1)}, u32[]{:S(2)}, u32[]{:S(2)}) collective-permute-start(bf16[4,2048]{1,0:T(4,128)(2,1)S(1)} %get-tuple-element.50), channel_id=1, source_target_pairs={{0,1},{1,2},{2,3},{3,4},{4,5},{5,6},{6,7},{7,8},{8,9},{9,10},{10,1... | collective-permute-start | bytes 49160 | tf_op jit(solution)/shard_map/ppermute | solution.py:16
  42.5 1.8 collective-permute-done.5
  46.2 2.2 reshape.262
  51.1 4.8 %collective-permute-start.6 = (bf16[4,2048]{1,0:T(4,128)(2,1)S(1)}, bf16[4,2048]{1,0:T(4,128)(2,1)S(1)}, u32[]{:S(2)}, u32[]{:S(2)}) collective-permute-start(bf16[4,2048]{1,0:T(4,128)(2,1)S(1)} %get-tuple-element.48), channel_id=1, source_target_pairs={{0,1},{1,2},{2,3},{3,4},{4,5},{5,6},{6,7},{7,8},{8,9},{9,10},{10,1... | collective-permute-start | bytes 49160 | tf_op jit(solution)/shard_map/ppermute | solution.py:16
  56.0 1.8 collective-permute-start.7
  62.9 2.2 reshape.265
  68.0 41.0 %all-gather.9.cloned.1.call-done = f32[2048,128]{1,0:T(8,128)} async-done(((f32[128,128]{1,0:T(8,128)}), f32[2048,128]{1,0:T(8,128)}) %all-gather.9.cloned.1.call-update) | async-done | bytes 1048592 | tf_op jit(solution)/shard_map/all_gather | solution.py:49
  110.5 8.8 %cholesky.74 = f32[96,96]{1,0:T(8,128)S(1)} custom-call(f32[96,96]{1,0:T(8,128)S(1)} %fusion.107), custom_call_target="Cholesky" | custom-call | tf_op jit(solution)/shard_map/jit(cholesky)/cholesky | solution.py:68
  120.6 7.4 %custom-call.10 = f32[1,96,96]{1,2,0:T(8,128)S(1)} custom-call(f32[1,96,96]{2,1,0:T(8,128)S(1)} %fusion.80), custom_call_target="InvertDiagBlocksLowerTriangular" | custom-call | tf_op jit(solution)/shard_map/jit(_cho_solve)/triangular_solve | solution.py:69
  130.7 2.2 collective-permute-start.8
  132.9 1.5 collective-permute-start.9
  134.4 1.6 collective-permute-done.9
  137.9 2.2 reshape.271
  142.8 4.2 collective-permute-start.10
  148.4 1.8 collective-permute-done.11
  155.3 4.6 collective-permute-start.12
  167.1 2.2 reshape.277
  172.7 40.5 %all-gather.11.cloned.1.call-done = f32[2048,128]{1,0:T(8,128)} async-done(((f32[128,128]{1,0:T(8,128)}), f32[2048,128]{1,0:T(8,128)}) %all-gather.11.cloned.1.call-update) | async-done | bytes 1048592 | tf_op jit(solution)/shard_map/all_gather | solution.py:49
  214.6 8.8 %cholesky.85 = f32[96,96]{1,0:T(8,128)S(1)} custom-call(f32[96,96]{1,0:T(8,128)S(1)} %fusion.103), custom_call_target="Cholesky" | custom-call | tf_op jit(solution)/shard_map/jit(cholesky)/cholesky | solution.py:68
  224.8 7.4 %custom-call.11 = f32[1,96,96]{1,2,0:T(8,128)S(1)} custom-call(f32[1,96,96]{2,1,0:T(8,128)S(1)} %fusion.81), custom_call_target="InvertDiagBlocksLowerTriangular" | custom-call | tf_op jit(solution)/shard_map/jit(_cho_solve)/triangular_solve | solution.py:69
  235.5 2.2 collective-permute-start.14
  239.0 1.8 collective-permute-done.15
  242.7 2.2 reshape.283
  249.3 4.2 collective-permute-start.16
  254.8 1.8 collective-permute-done.17
  258.5 2.2 reshape.286
  266.3 4.6 collective-permute-start.18
  271.0 1.7 collective-permute-start.19
  279.8 2.2 reshape.289
  285.2 40.7 %all-gather.13.cloned.1.call-done = f32[2048,128]{1,0:T(8,128)} async-done(((f32[128,128]{1,0:T(8,128)}), f32[2048,128]{1,0:T(8,128)}) %all-gather.13.cloned.1.call-update) | async-done | bytes 1048592 | tf_op jit(solution)/shard_map/all_gather | solution.py:49
  327.3 8.8 %cholesky.96 = f32[96,96]{1,0:T(8,128)S(1)} custom-call(f32[96,96]{1,0:T(8,128)S(1)} %fusion.99), custom_call_target="Cholesky" | custom-call | tf_op jit(solution)/shard_map/jit(cholesky)/cholesky | solution.py:68
  337.5 7.4 %custom-call.12 = f32[1,96,96]{1,2,0:T(8,128)S(1)} custom-call(f32[1,96,96]{2,1,0:T(8,128)S(1)} %fusion.82), custom_call_target="InvertDiagBlocksLowerTriangular" | custom-call | tf_op jit(solution)/shard_map/jit(_cho_solve)/triangular_solve | solution.py:69
  347.7 2.2 collective-permute-start.20
  349.8 1.5 collective-permute-start.21
  351.3 1.6 collective-permute-done.21
  354.8 2.2 reshape.295
  361.4 4.2 collective-permute-start.22
  367.0 1.8 collective-permute-done.23
  370.7 2.2 reshape.298
  378.4 4.6 collective-permute-start.24
  391.2 2.4 reshape.301
  407.1 30.4 %all-gather.15.cloned.1.call-done = f32[2048,128]{1,0:T(8,128)} async-done(((f32[128,128]{1,0:T(8,128)}), f32[2048,128]{1,0:T(8,128)}) %all-gather.15.cloned.1.call-update) | async-done | bytes 1048592 | tf_op jit(solution)/shard_map/all_gather | solution.py:49
  439.0 8.8 %cholesky.107 = f32[96,96]{1,0:T(8,128)S(1)} custom-call(f32[96,96]{1,0:T(8,128)S(1)} %fusion.95), custom_call_target="Cholesky" | custom-call | tf_op jit(solution)/shard_map/jit(cholesky)/cholesky | solution.py:68
  449.1 7.4 %custom-call.13 = f32[1,96,96]{1,2,0:T(8,128)S(1)} custom-call(f32[1,96,96]{2,1,0:T(8,128)S(1)} %fusion.83), custom_call_target="InvertDiagBlocksLowerTriangular" | custom-call | tf_op jit(solution)/shard_map/jit(_cho_solve)/triangular_solve | solution.py:69
  (472 shorter events, 138.8 us)
Async XLA Ops:
  7.2 101.8 %all-gather.9.cloned.1.call-start = ((), (), s32[]{:S(2)}) async-start(), calls=%async_computation | async-start | bytes 1114112 | tf_op jit(solution)/shard_map/all_gather | solution.py:49
  8.0 43.0 %copy-start.48 = (pred[2,4]{1,0:T(4,128)(4,1)}, pred[2,4]{1,0:T(4,128)(4,1)S(1)}, u32[]{:S(2)}) copy-start(pred[2,4]{1,0:T(4,128)(4,1)S(1)} %compare_bitcast_fusion) | copy-start | bytes 28
  8.8 42.2 %copy-start.65 = (pred[8]{0:T(512)(128)(4,1)}, pred[8]{0:T(512)(128)(4,1)S(1)}, u32[]{:S(2)}) copy-start(pred[8]{0:T(512)(128)(4,1)S(1)} %compare_and_fusion.1) | copy-start | bytes 28
  10.5 4.7 collective-permute-start
  12.9 5.2 %collective-permute-start.1 = (bf16[4,2048]{1,0:T(4,128)(2,1)S(1)}, bf16[4,2048]{1,0:T(4,128)(2,1)S(1)}, u32[]{:S(2)}, u32[]{:S(2)}) collective-permute-start(bf16[4,2048]{1,0:T(4,128)(2,1)S(1)} %get-tuple-element.55), channel_id=1, source_target_pairs={{1,0},{2,1},{3,2},{4,3},{5,4},{6,5},{7,6},{8,7},{9,8},{10,9},{11,1... | collective-permute-start | bytes 49160 | tf_op jit(solution)/shard_map/ppermute | solution.py:16
  15.0 47.0 %copy-start.72 = (pred[96]{0:T(512)(128)(4,1)}, pred[96]{0:T(512)(128)(4,1)S(1)}, u32[]{:S(2)}) copy-start(pred[96]{0:T(512)(128)(4,1)S(1)} %compare_and_fusion) | copy-start | bytes 292
  15.2 45.8 %copy-start.55 = (bf16[25]{0:T(256)(128)(2,1)}, bf16[25]{0:T(256)(128)(2,1)S(1)}, u32[]{:S(2)}) copy-start(bf16[25]{0:T(256)(128)(2,1)S(1)} %pad.91.clone) | copy-start | bytes 154
  23.2 34.6 %copy-start.11 = (f32[16,2048]{1,0:T(8,128)}, f32[16,2048]{1,0:T(8,128)S(1)}, u32[]{:S(2)}) copy-start(f32[16,2048]{1,0:T(8,128)S(1)} %get-tuple-element.13) | copy-start | bytes 393220
  24.0 5.7 %collective-permute-start.2 = (bf16[4,2048]{1,0:T(4,128)(2,1)S(1)}, bf16[4,2048]{1,0:T(4,128)(2,1)S(1)}, u32[]{:S(2)}, u32[]{:S(2)}) collective-permute-start(bf16[4,2048]{1,0:T(4,128)(2,1)S(1)} %get-tuple-element.52), channel_id=1, source_target_pairs={{0,1},{1,2},{2,3},{3,4},{4,5},{5,6},{6,7},{7,8},{8,9},{9,10},{10,1... | collective-permute-start | bytes 49160 | tf_op jit(solution)/shard_map/ppermute | solution.py:16
  28.4 3.1 collective-permute-start.3
  36.5 6.0 %collective-permute-start.4 = (bf16[4,2048]{1,0:T(4,128)(2,1)S(1)}, bf16[4,2048]{1,0:T(4,128)(2,1)S(1)}, u32[]{:S(2)}, u32[]{:S(2)}) collective-permute-start(bf16[4,2048]{1,0:T(4,128)(2,1)S(1)} %get-tuple-element.50), channel_id=1, source_target_pairs={{0,1},{1,2},{2,3},{3,4},{4,5},{5,6},{6,7},{7,8},{8,9},{9,10},{10,1... | collective-permute-start | bytes 49160 | tf_op jit(solution)/shard_map/ppermute | solution.py:16
  41.2 3.1 collective-permute-start.5
  51.1 9.9 %collective-permute-start.6 = (bf16[4,2048]{1,0:T(4,128)(2,1)S(1)}, bf16[4,2048]{1,0:T(4,128)(2,1)S(1)}, u32[]{:S(2)}, u32[]{:S(2)}) collective-permute-start(bf16[4,2048]{1,0:T(4,128)(2,1)S(1)} %get-tuple-element.48), channel_id=1, source_target_pairs={{0,1},{1,2},{2,3},{3,4},{4,5},{5,6},{6,7},{7,8},{8,9},{9,10},{10,1... | collective-permute-start | bytes 49160 | tf_op jit(solution)/shard_map/ppermute | solution.py:16
  56.0 5.0 %collective-permute-start.7 = (bf16[4,2048]{1,0:T(4,128)(2,1)S(1)}, bf16[4,2048]{1,0:T(4,128)(2,1)S(1)}, u32[]{:S(2)}, u32[]{:S(2)}) collective-permute-start(bf16[4,2048]{1,0:T(4,128)(2,1)S(1)} %get-tuple-element.49), channel_id=1, source_target_pairs={{1,0},{2,1},{3,2},{4,3},{5,4},{6,5},{7,6},{8,7},{9,8},{10,9},{11,1... | collective-permute-start | bytes 49160 | tf_op jit(solution)/shard_map/ppermute | solution.py:16
  67.9 145.3 %all-gather.11.cloned.1.call-start = ((), (), s32[]{:S(2)}) async-start(), calls=%async_computation.1 | async-start | bytes 1114112 | tf_op jit(solution)/shard_map/all_gather | solution.py:49
  109.0 20.7 %copy-start.12 = (f32[16,2048]{1,0:T(8,128)S(1)}, f32[16,2048]{1,0:T(8,128)}, u32[]{:S(2)}) copy-start(f32[16,2048]{1,0:T(8,128)} %copy-done.11) | copy-start | bytes 393220
  110.3 20.2 %copy-start.49 = (pred[2,4]{1,0:T(4,128)(4,1)S(1)}, pred[2,4]{1,0:T(4,128)(4,1)}, u32[]{:S(2)}) copy-start(pred[2,4]{1,0:T(4,128)(4,1)} %copy-done.48) | copy-start | bytes 28
  110.5 25.5 %copy-start.56 = (bf16[25]{0:T(256)(128)(2,1)S(1)}, bf16[25]{0:T(256)(128)(2,1)}, u32[]{:S(2)}) copy-start(bf16[25]{0:T(256)(128)(2,1)} %copy-done.55) | copy-start | bytes 154
  130.7 3.6 collective-permute-start.8
  132.9 3.1 collective-permute-start.9
  142.8 5.6 %collective-permute-start.10 = (bf16[4,2048]{1,0:T(4,128)(2,1)S(1)}, bf16[4,2048]{1,0:T(4,128)(2,1)S(1)}, u32[]{:S(2)}, u32[]{:S(2)}) collective-permute-start(bf16[4,2048]{1,0:T(4,128)(2,1)S(1)} %get-tuple-element.44), channel_id=1, source_target_pairs={{0,1},{1,2},{2,3},{3,4},{4,5},{5,6},{6,7},{7,8},{8,9},{9,10},{10,1... | collective-permute-start | bytes 49160 | tf_op jit(solution)/shard_map/ppermute | solution.py:16
  147.1 3.1 collective-permute-start.11
  155.3 9.8 %collective-permute-start.12 = (bf16[4,2048]{1,0:T(4,128)(2,1)S(1)}, bf16[4,2048]{1,0:T(4,128)(2,1)S(1)}, u32[]{:S(2)}, u32[]{:S(2)}) collective-permute-start(bf16[4,2048]{1,0:T(4,128)(2,1)S(1)} %get-tuple-element.42), channel_id=1, source_target_pairs={{0,1},{1,2},{2,3},{3,4},{4,5},{5,6},{6,7},{7,8},{8,9},{9,10},{10,1... | collective-permute-start | bytes 49160 | tf_op jit(solution)/shard_map/ppermute | solution.py:16
  159.9 5.2 %collective-permute-start.13 = (bf16[4,2048]{1,0:T(4,128)(2,1)S(1)}, bf16[4,2048]{1,0:T(4,128)(2,1)S(1)}, u32[]{:S(2)}, u32[]{:S(2)}) collective-permute-start(bf16[4,2048]{1,0:T(4,128)(2,1)S(1)} %get-tuple-element.43), channel_id=1, source_target_pairs={{1,0},{2,1},{3,2},{4,3},{5,4},{6,5},{7,6},{8,7},{9,8},{10,9},{11,1... | collective-permute-start | bytes 49160 | tf_op jit(solution)/shard_map/ppermute | solution.py:16
  172.5 153.4 %all-gather.13.cloned.1.call-start = ((), (), s32[]{:S(2)}) async-start(), calls=%async_computation.2 | async-start | bytes 1114112 | tf_op jit(solution)/shard_map/all_gather | solution.py:49
  214.5 20.8 %copy-start.68 = (pred[8]{0:T(512)(128)(4,1)S(1)}, pred[8]{0:T(512)(128)(4,1)}, u32[]{:S(2)}) copy-start(pred[8]{0:T(512)(128)(4,1)} %copy-done.65) | copy-start | bytes 28
  214.5 20.9 %copy-start.51 = (pred[2,4]{1,0:T(4,128)(4,1)S(1)}, pred[2,4]{1,0:T(4,128)(4,1)}, u32[]{:S(2)}) copy-start(pred[2,4]{1,0:T(4,128)(4,1)} %copy-done.48) | copy-start | bytes 28
  214.6 26.2 %copy-start.59 = (bf16[25]{0:T(256)(128)(2,1)S(1)}, bf16[25]{0:T(256)(128)(2,1)}, u32[]{:S(2)}) copy-start(bf16[25]{0:T(256)(128)(2,1)} %copy-done.55) | copy-start | bytes 154
  235.5 3.5 collective-permute-start.14
  237.7 3.1 collective-permute-start.15
  249.3 5.6 %collective-permute-start.16 = (bf16[4,2048]{1,0:T(4,128)(2,1)S(1)}, bf16[4,2048]{1,0:T(4,128)(2,1)S(1)}, u32[]{:S(2)}, u32[]{:S(2)}) collective-permute-start(bf16[4,2048]{1,0:T(4,128)(2,1)S(1)} %get-tuple-element.38), channel_id=1, source_target_pairs={{0,1},{1,2},{2,3},{3,4},{4,5},{5,6},{6,7},{7,8},{8,9},{9,10},{10,1... | collective-permute-start | bytes 49160 | tf_op jit(solution)/shard_map/ppermute | solution.py:16
  253.5 3.1 collective-permute-start.17
  266.3 11.5 %collective-permute-start.18 = (bf16[4,2048]{1,0:T(4,128)(2,1)}, bf16[4,2048]{1,0:T(4,128)(2,1)S(1)}, u32[]{:S(2)}, u32[]{:S(2)}) collective-permute-start(bf16[4,2048]{1,0:T(4,128)(2,1)} %get-tuple-element.36), channel_id=1, source_target_pairs={{0,1},{1,2},{2,3},{3,4},{4,5},{5,6},{6,7},{7,8},{8,9},{9,10},{10,1... | collective-permute-start | bytes 49160 | tf_op jit(solution)/shard_map/ppermute | solution.py:16
  271.0 6.9 %collective-permute-start.19 = (bf16[4,2048]{1,0:T(4,128)(2,1)S(1)}, bf16[4,2048]{1,0:T(4,128)(2,1)S(1)}, u32[]{:S(2)}, u32[]{:S(2)}) collective-permute-start(bf16[4,2048]{1,0:T(4,128)(2,1)S(1)} %get-tuple-element.37), channel_id=1, source_target_pairs={{1,0},{2,1},{3,2},{4,3},{5,4},{6,5},{7,6},{8,7},{9,8},{10,9},{11,1... | collective-permute-start | bytes 49160 | tf_op jit(solution)/shard_map/ppermute | solution.py:16
  285.1 152.4 %all-gather.15.cloned.1.call-start = ((), (), s32[]{:S(2)}) async-start(), calls=%async_computation.3 | async-start | bytes 1114112 | tf_op jit(solution)/shard_map/all_gather | solution.py:49
  325.8 20.8 %copy-start.10 = (f32[16,2048]{1,0:T(8,128)S(1)}, f32[16,2048]{1,0:T(8,128)}, u32[]{:S(2)}) copy-start(f32[16,2048]{1,0:T(8,128)} %get-tuple-element.9) | copy-start | bytes 393220
  327.2 20.3 %copy-start.53 = (pred[2,4]{1,0:T(4,128)(4,1)S(1)}, pred[2,4]{1,0:T(4,128)(4,1)}, u32[]{:S(2)}) copy-start(pred[2,4]{1,0:T(4,128)(4,1)} %copy-done.48) | copy-start | bytes 28
  327.3 25.6 %copy-start.62 = (bf16[25]{0:T(256)(128)(2,1)S(1)}, bf16[25]{0:T(256)(128)(2,1)}, u32[]{:S(2)}) copy-start(bf16[25]{0:T(256)(128)(2,1)} %copy-done.55) | copy-start | bytes 154
  347.7 3.6 collective-permute-start.20
  349.8 3.1 collective-permute-start.21
  361.4 5.6 %collective-permute-start.22 = (bf16[4,2048]{1,0:T(4,128)(2,1)S(1)}, bf16[4,2048]{1,0:T(4,128)(2,1)S(1)}, u32[]{:S(2)}, u32[]{:S(2)}) collective-permute-start(bf16[4,2048]{1,0:T(4,128)(2,1)S(1)} %get-tuple-element.32), channel_id=1, source_target_pairs={{0,1},{1,2},{2,3},{3,4},{4,5},{5,6},{6,7},{7,8},{8,9},{9,10},{10,1... | collective-permute-start | bytes 49160 | tf_op jit(solution)/shard_map/ppermute | solution.py:16
  365.6 3.1 collective-permute-start.23
  378.4 10.8 %collective-permute-start.24 = (bf16[4,2048]{1,0:T(4,128)(2,1)}, bf16[4,2048]{1,0:T(4,128)(2,1)S(1)}, u32[]{:S(2)}, u32[]{:S(2)}) collective-permute-start(bf16[4,2048]{1,0:T(4,128)(2,1)} %get-tuple-element.30), channel_id=1, source_target_pairs={{0,1},{1,2},{2,3},{3,4},{4,5},{5,6},{6,7},{7,8},{8,9},{9,10},{10,1... | collective-permute-start | bytes 49160 | tf_op jit(solution)/shard_map/ppermute | solution.py:16
  383.1 6.2 %collective-permute-start.25 = (bf16[4,2048]{1,0:T(4,128)(2,1)S(1)}, bf16[4,2048]{1,0:T(4,128)(2,1)S(1)}, u32[]{:S(2)}, u32[]{:S(2)}) collective-permute-start(bf16[4,2048]{1,0:T(4,128)(2,1)S(1)} %get-tuple-element.31), channel_id=1, source_target_pairs={{1,0},{2,1},{3,2},{4,3},{5,4},{6,5},{7,6},{8,7},{9,8},{10,9},{11,1... | collective-permute-start | bytes 49160 | tf_op jit(solution)/shard_map/ppermute | solution.py:16
  406.7 50.3 %copy-start.25 = (f32[1024,32]{0,1:T(8,128)S(1)}, f32[1024,32]{0,1:T(8,128)}, u32[]{:S(2)}) copy-start(f32[1024,32]{0,1:T(8,128)} %copy.235) | copy-start | bytes 393220
  406.7 50.3 %copy-start.27 = (f32[1024,32]{0,1:T(8,128)S(1)}, f32[1024,32]{0,1:T(8,128)}, u32[]{:S(2)}) copy-start(f32[1024,32]{0,1:T(8,128)} %copy-done.26) | copy-start | bytes 393220
  406.9 50.1 %copy-start.29 = (f32[1024,32]{0,1:T(8,128)S(1)}, f32[1024,32]{0,1:T(8,128)}, u32[]{:S(2)}) copy-start(f32[1024,32]{0,1:T(8,128)} %copy-done.28) | copy-start | bytes 393220
  406.9 51.1 %copy-start.4 = (f32[1024,32]{1,0:T(8,128)S(1)}, f32[1024,32]{1,0:T(8,128)}, u32[]{:S(2)}) copy-start(f32[1024,32]{1,0:T(8,128)} %copy-done.3) | copy-start | bytes 393220
  (66 other events, 290.5 us)
Sparse Core Ops, SparseCore 0:
  68.1 40.9 all-gather.8
  172.6 40.5 all-gather.10
  285.2 40.5 all-gather.12
  396.9 40.5 all-gather.14
